TPU v7x, 256 devices: a whole 4x4x8 slice. The times are simulated.
256 devices in a mesh: seq: 32 (over x_lo, z, core), band: 8 (over y, x_hi).
Axes of the slice: x: 4 (x_hi: 2, x_lo: 2; x = x_hi * 2 + x_lo), y: 4, z: 8, core: 2. Of those that a mesh axis runs over, the one named last changes fastest.
Arguments:
- tokens: bfloat16 [4096, 1024], P('seq', 'band'), may hold values from -6 to 6
- mappable: int32 [4096], P('seq'), may hold values 0 or 1
- attn_gain: float32 [1024], replicated, may hold values from 0.1 to 1.9
- w_query: bfloat16 [1024, 1024], P(None, 'band'), may hold values from -1 to 1
- w_key: bfloat16 [1024, 1024], P(None, 'band'), may hold values from -4 to 4
- w_value: bfloat16 [1024, 1024], P(None, 'band'), may hold values from -0.1875 to 0.1875
- w_out: bfloat16 [1024, 1024], P('band'), may hold values from -0.75 to 0.75
- w_left: bfloat16 [1024, 128], replicated, may hold values from -0.1875 to 0.1875
- w_right: bfloat16 [1024, 128], replicated, may hold values from -0.1875 to 0.1875
- conv_gain: float32 [2, 128], replicated, may hold values from 0.1 to 1.9
- conv_kernel: bfloat16 [2, 3, 3, 128, 128], replicated, may hold values from -0.1875 to 0.1875
- conv_bias: float32 [2, 128], replicated, may hold values from -3 to 3
- contact_weight: float32 [128], replicated, may hold values from -0.5 to 0.5
Outputs:
- trunk_out: bfloat16 [4096, 1024], P('seq', 'band')
- contacts: float32 [4096, 256], P('seq', 'band')
All inputs are finite; a program needn't handle non-finite values. No bound on the sum of `mappable` on one device may be relied on, other than what follows from the above.
Results may differ from a plain program's by a relative error of at most 0.035.
Values may be sent and summed in bfloat16 or wider, within the bound.
A program may use at most 64 MiB of HBM per device.

v0:
```python
import jax
import jax.numpy as jnp
from jax import lax
from jax.sharding import PartitionSpec as P

HEAD = 128
CONVS = 2
DIAG = 32
epsilon = 1e-06


def passed_along(value, axis, steps):
    count = lax.axis_size(axis)
    initial, last = (max(0, -steps), min(count, count - steps))
    return lax.ppermute(value, axis, [(source, source + steps) for source in range(initial, last)])


def extended(x, sides, width):
    for axis, dim in sides:
        size, length = (lax.axis_size(axis), x.shape[dim])
        up = [(i, (i + 1) % size) for i in range(size - 1)]
        down = [(j, i) for i, j in up]
        last = lax.slice_in_dim(x, length - width, length, axis=dim)
        initial = lax.slice_in_dim(x, 0, width, axis=dim)
        before = lax.ppermute(last, axis, up)
        after = lax.ppermute(initial, axis, down)
        x = jnp.concatenate([before, x, after], axis=dim)
    return x


def rms_scale(values, gain):
    floats = values.astype(jnp.float32)
    return floats * lax.rsqrt(jnp.mean(floats * floats, axis=-1, keepdims=True) + epsilon) * gain


def shear_conv(padded, kernel, spread):
    out_rows = padded.shape[0] - 2 * spread
    out_diags = padded.shape[1] - 4 * spread
    windows = []
    for tap_row in range(3):
        for tap_col in range(3):
            row_first = spread * tap_row
            diag_first = 2 * spread + spread * (tap_col - tap_row)
            windows.append(
                padded[row_first : row_first + out_rows, diag_first : diag_first + out_diags]
            )
    stacked = jnp.concatenate(windows, axis=-1)
    flat_kernel = kernel.reshape(9 * kernel.shape[-2], kernel.shape[-1])
    return jnp.einsum("aek,kf->aef", stacked, flat_kernel, preferred_element_type=jnp.float32)


def valid_cells(row_first, diag_first, row_count, diag_count, length, band_width):
    rows_glob = row_first + jnp.arange(row_count, dtype=jnp.int32)
    diags_glob = diag_first + jnp.arange(diag_count, dtype=jnp.int32)
    inside = (
        (rows_glob[:, None] >= 0)
        & (rows_glob[:, None] < length)
        & (diags_glob[None, :] >= 0)
        & (diags_glob[None, :] < band_width)
        & (rows_glob[:, None] + diags_glob[None, :] < length)
    )
    return jnp.where(inside, 1.0, 0.0).astype(jnp.float32)[:, :, None]


def local(
    tokens,
    mappable,
    attn_gain,
    w_query,
    w_key,
    w_value,
    w_out,
    w_left,
    w_right,
    conv_gain,
    conv_kernel,
    conv_bias,
    contact_weight,
):
    row_count = tokens.shape[0]
    feature_share = tokens.shape[1]
    heads_here = w_query.shape[1] // HEAD
    seq_index = lax.axis_index("seq")
    band_index = lax.axis_index("band")
    length = row_count * lax.axis_size("seq")
    band_width = DIAG * lax.axis_size("band")
    gathered = lax.all_gather(tokens, "band", axis=1, tiled=True)
    normed = rms_scale(gathered, attn_gain).astype(jnp.bfloat16)
    query = jnp.dot(normed, w_query, preferred_element_type=jnp.float32).astype(jnp.bfloat16)
    key_rows = jnp.dot(normed, w_key, preferred_element_type=jnp.float32).astype(jnp.bfloat16)
    value = jnp.dot(normed, w_value, preferred_element_type=jnp.float32).astype(jnp.bfloat16)
    key_offset = ((mappable - 1).astype(jnp.float32) * 1000000000.0).astype(jnp.bfloat16)
    query_heads = query.reshape(row_count, heads_here, HEAD)
    row_top = jnp.full((heads_here, row_count), -jnp.inf, jnp.float32)
    weight_sum = jnp.zeros((heads_here, row_count), jnp.float32)
    mixed_sum = jnp.zeros((heads_here, row_count, HEAD), jnp.float32)
    key_piece = lax.all_gather(key_rows, "seq", axis=0, tiled=True)
    value_piece = lax.all_gather(value, "seq", axis=0, tiled=True)
    offset_piece = lax.all_gather(key_offset, "seq", axis=0, tiled=True)
    piece_rows = key_piece.shape[0]
    key_heads = key_piece.reshape(piece_rows, heads_here, HEAD)
    value_heads = value_piece.reshape(piece_rows, heads_here, HEAD)
    scores = (
        jnp.einsum("thd,nhd->htn", query_heads, key_heads, preferred_element_type=jnp.float32)
        * HEAD ** (-0.5)
        + offset_piece.astype(jnp.float32)[None, None, :]
    )
    new_top = jnp.max(scores, axis=2)
    weights = jnp.exp(scores - new_top[:, :, None])
    fade = jnp.exp(row_top - new_top)
    weight_sum = weight_sum * fade + jnp.sum(weights, axis=2)
    mixed_sum = mixed_sum * fade[:, :, None] + jnp.einsum(
        "htn,nhd->htd",
        weights.astype(jnp.bfloat16),
        value_heads,
        preferred_element_type=jnp.float32,
    )
    row_top, weight_sum, mixed_sum = (new_top, weight_sum, mixed_sum)
    attended = (
        (mixed_sum / weight_sum[:, :, None])
        .astype(jnp.bfloat16)
        .transpose(1, 0, 2)
        .reshape(row_count, heads_here * HEAD)
    )
    projected = jnp.dot(attended, w_out, preferred_element_type=jnp.float32)
    keep_rows = mappable.astype(jnp.bfloat16)[:, None]
    summed = lax.psum_scatter(
        projected.astype(jnp.bfloat16), "band", scatter_dimension=1, tiled=True
    ).astype(jnp.float32)
    trunk_out = (tokens.astype(jnp.float32) + summed).astype(jnp.bfloat16)
    rows_left = lax.dynamic_slice_in_dim(w_left, band_index * feature_share, feature_share, 0)
    rows_right = lax.dynamic_slice_in_dim(w_right, band_index * feature_share, feature_share, 0)
    part_left, part_right = (
        lax.psum(
            jnp.dot(trunk_out, rows_left, preferred_element_type=jnp.float32).astype(jnp.bfloat16),
            "band",
        ).astype(jnp.float32),
        lax.psum(
            jnp.dot(trunk_out, rows_right, preferred_element_type=jnp.float32).astype(jnp.bfloat16),
            "band",
        ).astype(jnp.float32),
    )
    left_side = part_left.astype(jnp.bfloat16) * keep_rows
    right_side = part_right.astype(jnp.bfloat16) * keep_rows
    row_start = seq_index * row_count
    diag_start = band_index * DIAG
    span_rows = row_count + DIAG
    following = passed_along(right_side, "seq", -1)
    window = jnp.concatenate([right_side, following], axis=0)
    block_reach = band_index * DIAG // row_count
    most_reach = (lax.axis_size("band") - 1) * DIAG // row_count

    def advance(turn_index, carry):
        current, chosen = carry
        current = passed_along(current, "seq", -1)
        chosen = jnp.where(block_reach == turn_index + 1, current, chosen)
        return (current, chosen)

    window = lax.fori_loop(0, most_reach, advance, (window, window))[1]
    first_row = band_index * DIAG % row_count
    window_rows = lax.dynamic_slice_in_dim(window, first_row, span_rows, 0)
    repeated = jnp.tile(window_rows, (row_count + 1, 1))[: row_count * (span_rows + 1)]
    hankel_rows = repeated.reshape(row_count, span_rows + 1, window_rows.shape[1])[:, :DIAG]
    pair_field = (
        left_side[:, None, :].astype(jnp.float32)
        * hankel_rows.astype(jnp.float32)
        * valid_cells(row_start, diag_start, row_count, DIAG, length, band_width)
    ).astype(jnp.bfloat16)
    tile_valid = valid_cells(row_start, diag_start, row_count, DIAG, length, band_width)
    for layer_index in range(CONVS):
        spread = 2**layer_index
        activated = jax.nn.gelu(rms_scale(pair_field, conv_gain[layer_index])).astype(jnp.bfloat16)
        padded = extended(activated, (("seq", 0), ("band", 1)), 2 * spread)
        padded = padded[spread : padded.shape[0] - spread]
        conv_term = shear_conv(padded, conv_kernel[layer_index], spread)
        pair_field = (
            (pair_field.astype(jnp.float32) + conv_term + conv_bias[layer_index]) * tile_valid
        ).astype(jnp.bfloat16)
    contacts = jnp.sum(pair_field.astype(jnp.float32) * contact_weight, axis=-1)
    return (trunk_out, contacts)


def solution(mesh):
    return jax.shard_map(
        local,
        mesh=mesh,
        in_specs=(
            P("seq", "band"),
            P("seq"),
            P(),
            P(None, "band"),
            P(None, "band"),
            P(None, "band"),
            P("band", None),
            P(),
            P(),
            P(),
            P(),
            P(),
            P(),
        ),
        out_specs=(P("seq", "band"), P("seq", "band")),
        check_vma=False,
    )
```

profile of v0, /device:TPU:2, one launch (start us, length us, event | category | flops | bytes accessed | tf_op | source)
XLA Modules:
  0.0 438.1 jit_solution(7441531402315791843)
XLA Ops:
  7.2 32.2 %all_gather.12 = bf16[128,1024]{1,0:T(8,128)(2,1)S(1)} all-gather(bf16[128,128]{1,0:T(8,128)(2,1)} %param.13), channel_id=1, replica_groups=mesh['seq'=32,'band'=8] {'band'}, dimensions={1}, use_global_device_ids=true | all-gather | bytes 294912 | tf_op jit(solution)/shard_map/all_gather | solution.py:87
  41.5 1.9 convolution_convert_fusion.3
  44.1 35.9 %all-gather = bf16[32,1,128]{2,1,0:T(2,128)(2,1)S(1)} all-gather(bf16[1,1,128]{2,1,0:T(2,128)(2,1)S(1)} %convert_bitcast_fusion), channel_id=1, replica_groups=mesh['seq'=32,'band'=8] {'seq'}, dimensions={0}, use_global_device_ids=true | all-gather | bytes 8448 | tf_op jit(solution)/shard_map/all_gather | solution.py:99
  80.1 25.7 %all-gather.4.cloned.1.call-done = bf16[4096,128]{1,0:T(8,128)(2,1)} async-done(((bf16[128,128]{1,0:T(8,128)(2,1)}), bf16[4096,128]{1,0:T(8,128)(2,1)}) %all-gather.4.cloned.1.call-update) | async-done | bytes 1048592 | tf_op jit(solution)/shard_map/all_gather | solution.py:97
  105.8 2.0 fusion.60
  108.3 63.3 %all-gather.6.cloned.1.call-done = bf16[4096,128]{1,0:T(8,128)(2,1)} async-done(((bf16[128,128]{1,0:T(8,128)(2,1)}), bf16[4096,128]{1,0:T(8,128)(2,1)}) %all-gather.6.cloned.1.call-update) | async-done | bytes 1048592 | tf_op jit(solution)/shard_map/all_gather | solution.py:98
  171.6 2.0 convolution_convert_fusion
  174.6 75.3 %reduce-scatter.4.cloned.1.call-done = bf16[128,128]{1,0:T(8,128)(2,1)} async-done(((bf16[1024,128]{1,0:T(8,128)(2,1)}), bf16[128,128]{1,0:T(8,128)(2,1)}) %reduce-scatter.4.cloned.1.call-update) | async-done | bytes 32784
  253.8 87.3 %all-reduce.3.cloned.1.call-done = (bf16[128,128]{1,0:T(8,128)(2,1)}, bf16[128,128]{1,0:T(8,128)(2,1)}) async-done(((bf16[128,128]{1,0:T(8,128)(2,1)}, bf16[128,128]{1,0:T(8,128)(2,1)}), (bf16[128,128]{1,0:T(8,128)(2,1)}, bf16[128,128]{1,0:T(8,128)(2,1)})) %all-reduce.3.cloned.1.call-update) | async-done | bytes 65552 | tf_op jit(solution)/shard_map/psum | solution.py:138
  342.0 1.9 collective-permute-start
  345.5 5.7 %collective-permute-start.1 = (bf16[256,128]{1,0:T(8,128)(2,1)S(1)}, bf16[256,128]{1,0:T(8,128)(2,1)S(1)}, u32[]{:S(2)}, u32[]{:S(2)}) collective-permute-start(bf16[256,128]{1,0:T(8,128)(2,1)S(1)} %pad_maximum_fusion.9), channel_id=1, source_target_pairs={{8,0},{16,8},{24,16},{32,24},{40,32},{48,40},{56,48},{64,56},{72,6... | collective-permute-start | bytes 196616 | tf_op jit(solution)/shard_map/while/body/eval_jaxpr/ppermute | solution.py:15
  354.0 2.7 slice.172
  356.7 7.7 %reshape.195 = bf16[128,161,128]{2,1,0:T(8,128)(2,1)} reshape(bf16[20608,128]{1,0:T(8,128)(2,1)} %slice.172) | data formatting | bytes 10551296 | tf_op jit(solution)/shard_map/reshape | solution.py:163
  369.2 1.9 collective-permute-start.2
  371.1 5.8 %collective-permute-start.3 = (bf16[2,32,128]{2,0,1:T(2,128)(2,1)S(1)}, bf16[2,32,128]{2,0,1:T(2,128)(2,1)S(1)}, u32[]{:S(2)}, u32[]{:S(2)}) collective-permute-start(bf16[2,32,128]{2,0,1:T(2,128)(2,1)S(1)} %get-tuple-element.29), channel_id=1, source_target_pairs={{8,0},{16,8},{24,16},{32,24},{40,32},{48,40},{56,48},{64,56},{72,6... | collective-permute-start | bytes 49160 | tf_op jit(solution)/shard_map/ppermute | solution.py:26
  378.4 1.9 collective-permute-start.5
  382.2 5.8 %collective-permute-done.4 = bf16[132,2,128]{2,0,1:T(8,128)(2,1)S(1)} collective-permute-done((bf16[132,2,128]{2,0,1:T(8,128)(2,1)S(1)}, bf16[132,2,128]{2,0,1:T(8,128)(2,1)S(1)}, u32[]{:S(2)}, u32[]{:S(2)}) %collective-permute-start.4) | collective-permute-done | bytes 67616 | tf_op jit(solution)/shard_map/ppermute | solution.py:26
  390.0 1.9 constant_dynamic-update-slice_fusion
  394.1 3.6 fusion.14
  398.8 1.9 collective-permute-start.6
  400.8 5.8 %collective-permute-start.7 = (bf16[4,32,128]{2,0,1:T(4,128)(2,1)S(1)}, bf16[4,32,128]{2,0,1:T(4,128)(2,1)S(1)}, u32[]{:S(2)}, u32[]{:S(2)}) collective-permute-start(bf16[4,32,128]{2,0,1:T(4,128)(2,1)S(1)} %get-tuple-element.27), channel_id=1, source_target_pairs={{8,0},{16,8},{24,16},{32,24},{40,32},{48,40},{56,48},{64,56},{72,6... | collective-permute-start | bytes 98312 | tf_op jit(solution)/shard_map/ppermute | solution.py:26
  408.2 5.8 %collective-permute-start.9 = (bf16[136,4,128]{2,0,1:T(8,128)(2,1)S(1)}, bf16[136,4,128]{2,0,1:T(8,128)(2,1)S(1)}, u32[]{:S(2)}, u32[]{:S(2)}) collective-permute-start(bf16[136,4,128]{2,0,1:T(8,128)(2,1)S(1)} %get-tuple-element.21), channel_id=1, source_target_pairs={{0,1},{1,2},{2,3},{3,4},{4,5},{5,6},{6,7},{8,9},{9,10},{10,11},{11... | collective-permute-start | bytes 417800 | tf_op jit(solution)/shard_map/ppermute | solution.py:25
  416.6 5.9 %collective-permute-done.8 = bf16[136,4,128]{2,0,1:T(8,128)(2,1)S(1)} collective-permute-done((bf16[136,4,128]{2,0,1:T(8,128)(2,1)S(1)}, bf16[136,4,128]{2,0,1:T(8,128)(2,1)S(1)}, u32[]{:S(2)}, u32[]{:S(2)}) %collective-permute-start.8) | collective-permute-done | bytes 139296 | tf_op jit(solution)/shard_map/ppermute | solution.py:26
  428.0 3.5 multiply_reduce_fusion
  (90 shorter events, 36.3 us)
Async XLA Ops:
  7.2 98.6 %copy-start = (bf16[1024,128]{1,0:T(8,128)(2,1)S(1)}, bf16[1024,128]{1,0:T(8,128)(2,1)}, u32[]{:S(2)}) copy-start(bf16[1024,128]{1,0:T(8,128)(2,1)} %param.16) | copy-start | bytes 786436
  7.2 98.6 %all-gather.4.cloned.1.call-start = ((), (), s32[]{:S(2)}) async-start(), calls=%async_computation.1 | async-start | bytes 1081344 | tf_op jit(solution)/shard_map/all_gather | solution.py:97
  41.5 130.1 %all-gather.6.cloned.1.call-start = ((), (), s32[]{:S(2)}) async-start(), calls=%async_computation.2 | async-start | bytes 1081344 | tf_op jit(solution)/shard_map/all_gather | solution.py:98
  43.4 206.4 %reduce-scatter.4.cloned.1.call-start = ((), (), s32[]{:S(2)}) async-start(), calls=%async_computation.3 | async-start | bytes 294912
  105.8 65.8 %copy-start.3 = (bf16[128,1024]{1,0:T(8,128)(2,1)S(1)}, bf16[128,1024]{1,0:T(8,128)(2,1)}, u32[]{:S(2)}) copy-start(bf16[128,1024]{1,0:T(8,128)(2,1)} %param.19) | copy-start | bytes 786436
  171.6 2.9 copy-start.7
  171.6 3.0 copy-start.1
  171.6 79.2 %copy-start.4 = (bf16[128,128]{1,0:T(8,128)(2,1)S(1)}, bf16[128,128]{1,0:T(8,128)(2,1)}, u32[]{:S(2)}) copy-start(bf16[128,128]{1,0:T(8,128)(2,1)} %param.13) | copy-start | bytes 98308
  173.5 177.7 %copy-start.5 = (f32[2,128]{1,0:T(2,128)S(1)}, f32[2,128]{1,0:T(2,128)}, u32[]{:S(2)}) copy-start(f32[2,128]{1,0:T(2,128)} %param.22) | copy-start | bytes 3076
  174.4 166.7 %all-reduce.3.cloned.1.call-start = ((), (), s32[]{:S(2)}) async-start(), calls=%async_computation.4 | async-start | bytes 131072 | tf_op jit(solution)/shard_map/psum | solution.py:138
  250.8 103.2 %copy-start.2 = (bf16[128,128]{1,0:T(8,128)(2,1)}, bf16[128,128]{1,0:T(8,128)(2,1)S(1)}, u32[]{:S(2)}) copy-start(bf16[128,128]{1,0:T(8,128)(2,1)S(1)} %add_convert_fusion) | copy-start | bytes 98308
  342.0 3.5 collective-permute-start
  345.5 7.6 %collective-permute-start.1 = (bf16[256,128]{1,0:T(8,128)(2,1)S(1)}, bf16[256,128]{1,0:T(8,128)(2,1)S(1)}, u32[]{:S(2)}, u32[]{:S(2)}) collective-permute-start(bf16[256,128]{1,0:T(8,128)(2,1)S(1)} %pad_maximum_fusion.9), channel_id=1, source_target_pairs={{8,0},{16,8},{24,16},{32,24},{40,32},{48,40},{56,48},{64,56},{72,6... | collective-permute-start | bytes 196616 | tf_op jit(solution)/shard_map/while/body/eval_jaxpr/ppermute | solution.py:15
  365.7 11.2 %copy-start.6 = (f32[2,128]{1,0:T(2,128)S(1)}, f32[2,128]{1,0:T(2,128)}, u32[]{:S(2)}) copy-start(f32[2,128]{1,0:T(2,128)} %param.24) | copy-start | bytes 3076
  369.2 7.8 %collective-permute-start.2 = (bf16[2,32,128]{2,0,1:T(2,128)(2,1)S(1)}, bf16[2,32,128]{2,0,1:T(2,128)(2,1)S(1)}, u32[]{:S(2)}, u32[]{:S(2)}) collective-permute-start(bf16[2,32,128]{2,0,1:T(2,128)(2,1)S(1)} %get-tuple-element.30), channel_id=1, source_target_pairs={{0,8},{8,16},{16,24},{24,32},{32,40},{40,48},{48,56},{56,64},{64,7... | collective-permute-start | bytes 49160 | tf_op jit(solution)/shard_map/ppermute | solution.py:25
  371.1 7.2 %collective-permute-start.3 = (bf16[2,32,128]{2,0,1:T(2,128)(2,1)S(1)}, bf16[2,32,128]{2,0,1:T(2,128)(2,1)S(1)}, u32[]{:S(2)}, u32[]{:S(2)}) collective-permute-start(bf16[2,32,128]{2,0,1:T(2,128)(2,1)S(1)} %get-tuple-element.29), channel_id=1, source_target_pairs={{8,0},{16,8},{24,16},{32,24},{40,32},{48,40},{56,48},{64,56},{72,6... | collective-permute-start | bytes 49160 | tf_op jit(solution)/shard_map/ppermute | solution.py:26
  378.4 3.9 collective-permute-start.5
  380.3 7.7 %collective-permute-start.4 = (bf16[132,2,128]{2,0,1:T(8,128)(2,1)S(1)}, bf16[132,2,128]{2,0,1:T(8,128)(2,1)S(1)}, u32[]{:S(2)}, u32[]{:S(2)}) collective-permute-start(bf16[132,2,128]{2,0,1:T(8,128)(2,1)S(1)} %get-tuple-element.26), channel_id=1, source_target_pairs={{1,0},{2,1},{3,2},{4,3},{5,4},{6,5},{7,6},{9,8},{10,9},{11,10},{12... | collective-permute-start | bytes 202760 | tf_op jit(solution)/shard_map/ppermute | solution.py:26
  398.8 7.7 %collective-permute-start.6 = (bf16[4,32,128]{2,0,1:T(4,128)(2,1)S(1)}, bf16[4,32,128]{2,0,1:T(4,128)(2,1)S(1)}, u32[]{:S(2)}, u32[]{:S(2)}) collective-permute-start(bf16[4,32,128]{2,0,1:T(4,128)(2,1)S(1)} %get-tuple-element.28), channel_id=1, source_target_pairs={{0,8},{8,16},{16,24},{24,32},{32,40},{40,48},{48,56},{56,64},{64,7... | collective-permute-start | bytes 98312 | tf_op jit(solution)/shard_map/ppermute | solution.py:25
  400.8 7.3 %collective-permute-start.7 = (bf16[4,32,128]{2,0,1:T(4,128)(2,1)S(1)}, bf16[4,32,128]{2,0,1:T(4,128)(2,1)S(1)}, u32[]{:S(2)}, u32[]{:S(2)}) collective-permute-start(bf16[4,32,128]{2,0,1:T(4,128)(2,1)S(1)} %get-tuple-element.27), channel_id=1, source_target_pairs={{8,0},{16,8},{24,16},{32,24},{40,32},{48,40},{56,48},{64,56},{72,6... | collective-permute-start | bytes 98312 | tf_op jit(solution)/shard_map/ppermute | solution.py:26
  408.2 8.4 %collective-permute-start.9 = (bf16[136,4,128]{2,0,1:T(8,128)(2,1)S(1)}, bf16[136,4,128]{2,0,1:T(8,128)(2,1)S(1)}, u32[]{:S(2)}, u32[]{:S(2)}) collective-permute-start(bf16[136,4,128]{2,0,1:T(8,128)(2,1)S(1)} %get-tuple-element.21), channel_id=1, source_target_pairs={{0,1},{1,2},{2,3},{3,4},{4,5},{5,6},{6,7},{8,9},{9,10},{10,11},{11... | collective-permute-start | bytes 417800 | tf_op jit(solution)/shard_map/ppermute | solution.py:25
  414.0 8.5 %collective-permute-start.8 = (bf16[136,4,128]{2,0,1:T(8,128)(2,1)S(1)}, bf16[136,4,128]{2,0,1:T(8,128)(2,1)S(1)}, u32[]{:S(2)}, u32[]{:S(2)}) collective-permute-start(bf16[136,4,128]{2,0,1:T(8,128)(2,1)S(1)} %get-tuple-element.22), channel_id=1, source_target_pairs={{1,0},{2,1},{3,2},{4,3},{5,4},{6,5},{7,6},{9,8},{10,9},{11,10},{12... | collective-permute-start | bytes 417800 | tf_op jit(solution)/shard_map/ppermute | solution.py:26
  426.8 1.2 copy-start.8
Sparse Core Ops, SparseCore 0:
  41.6 64.1 all-gather.3
  108.2 63.2 all-gather.5
  175.4 74.4 reduce-scatter.3
  253.9 87.1 all-reduce.2
where the time goes:
time: 439 us; the launch traced here: 438 us
  waiting for transfers between devices  270 us (62%)
  blocking collectives  68.2 us (16%)
  starting transfers between devices  33.9 us (8%)
  local copies, waits for them, and re-layouts  20.2 us (5%)
  matrix products  17.8 us (4%)
  between operations  14.3 us (3%)
  other arithmetic  13.3 us (3%)
    psum x1, waiting for transfers between devices, local(): lax.psum(jnp.dot(trunk_out, rows_right, preferred_element_type=jnp.float3...  87.3 us
    unnamed x5, waiting for transfers between devices  75.3 us
    all_gather x1, waiting for transfers between devices, local(): value_piece = lax.all_gather(value, 'seq', axis=0, tiled=True)  63.3 us
    all_gather x1, blocking collectives, local(): offset_piece = lax.all_gather(key_offset, 'seq', axis=0, tiled=True)  35.9 us
    all_gather x1, blocking collectives, local(): gathered = lax.all_gather(tokens, 'band', axis=1, tiled=True)  32.2 us
    all_gather x1, waiting for transfers between devices, local(): key_piece = lax.all_gather(key_rows, 'seq', axis=0, tiled=True)  25.7 us
    ppermute x4, waiting for transfers between devices, extended(): after = lax.ppermute(initial, axis, down)  14.6 us
    ppermute x4, starting transfers between devices, extended(): after = lax.ppermute(initial, axis, down)  14.5 us
  transfers between devices with their start and end apart: 14, of which 12 were waited for; matrix products, arithmetic and copies ran while one was open for 1% of the time, Pallas kernels for 0%

commit v1 on v0

--- a/solution.py
+++ b/solution.py
@@ -2,6 +2,7 @@
 import jax.numpy as jnp
 from jax import lax
 from jax.sharding import PartitionSpec as P
+from jax.lax import all_gather
 
 HEAD = 128
 CONVS = 2
@@ -135,9 +136,14 @@
             jnp.dot(trunk_out, rows_left, preferred_element_type=jnp.float32).astype(jnp.bfloat16),
             "band",
         ).astype(jnp.float32),
-        lax.psum(
-            jnp.dot(trunk_out, rows_right, preferred_element_type=jnp.float32).astype(jnp.bfloat16),
-            "band",
+        jnp.sum(
+            all_gather(
+                jnp.dot(trunk_out, rows_right, preferred_element_type=jnp.float32).astype(
+                    jnp.bfloat16
+                ),
+                "band",
+            ),
+            axis=0,
         ).astype(jnp.float32),
     )
     left_side = part_left.astype(jnp.bfloat16) * keep_rows

time: 439 us -> 423 us (0.964)
  waiting for transfers between devices: 270 us -> 183 us
  blocking collectives: 68.2 us -> 143 us
    psum x1 -> x0, waiting for transfers between devices: 87.3 us -> none  [local(): lax.psum(jnp.dot(trunk_out, rows_right, preferred_element_type=jnp.float3...]
    psum x0 -> x1, blocking collectives: none -> 39.7 us  [local(): lax.psum(jnp.dot(trunk_out, rows_left, preferred_element_type=jnp.float32...]
    all_gather x0 -> x1, blocking collectives: none -> 34.7 us  [local(): all_gather(jnp.dot(trunk_out, rows_right, preferred_element_type=jnp.floa...]
    unnamed x5 -> x4, waiting for transfers between devices: 75.3 us -> 75.4 us
  transfers between devices with their start and end apart: 14 -> 13, of which waited for: 12 -> 11; matrix products, arithmetic and copies ran while one was open for 1% -> 1% of each run, Pallas kernels for 0% -> 0%
where the time goes in v1:
time: 423 us; the launch traced here: 422 us
  waiting for transfers between devices  183 us (43%)
  blocking collectives  143 us (34%)
  starting transfers between devices  33.2 us (8%)
  local copies, waits for them, and re-layouts  20.3 us (5%)
  matrix products  16.6 us (4%)
  between operations  14.3 us (3%)
  other arithmetic  12.6 us (3%)
    unnamed x4, waiting for transfers between devices  75.4 us
    all_gather x1, waiting for transfers between devices, local(): value_piece = lax.all_gather(value, 'seq', axis=0, tiled=True)  63.3 us
    psum x1, blocking collectives, local(): lax.psum(jnp.dot(trunk_out, rows_left, preferred_element_type=jnp.float32...  39.7 us
    all_gather x1, blocking collectives, local(): offset_piece = lax.all_gather(key_offset, 'seq', axis=0, tiled=True)  35.9 us
    all_gather x1, blocking collectives, local(): all_gather(jnp.dot(trunk_out, rows_right, preferred_element_type=jnp.floa...  34.7 us
    all_gather x1, blocking collectives, local(): gathered = lax.all_gather(tokens, 'band', axis=1, tiled=True)  32.2 us
    all_gather x1, waiting for transfers between devices, local(): key_piece = lax.all_gather(key_rows, 'seq', axis=0, tiled=True)  25.7 us
    ppermute x4, waiting for transfers between devices, extended(): after = lax.ppermute(initial, axis, down)  14.6 us
  transfers between devices with their start and end apart: 13, of which 11 were waited for; matrix products, arithmetic and copies ran while one was open for 1% of the time, Pallas kernels for 0%

profile of v1, /device:TPU:2, one launch (start us, length us, event | category | flops | bytes accessed | tf_op | source)
XLA Modules:
  0.0 422.4 jit_solution(5975733706799160766)
XLA Ops:
  7.2 32.2 %all_gather.18 = bf16[128,1024]{1,0:T(8,128)(2,1)S(1)} all-gather(bf16[128,128]{1,0:T(8,128)(2,1)} %param.13), channel_id=1, replica_groups=mesh['seq'=32,'band'=8] {'band'}, dimensions={1}, use_global_device_ids=true | all-gather | bytes 294912 | tf_op jit(solution)/shard_map/all_gather | solution.py:88
  41.5 1.9 convolution_convert_fusion.3
  44.1 35.9 %all-gather.1 = bf16[32,1,128]{2,1,0:T(2,128)(2,1)S(1)} all-gather(bf16[1,1,128]{2,1,0:T(2,128)(2,1)S(1)} %convert_bitcast_fusion), channel_id=1, replica_groups=mesh['seq'=32,'band'=8] {'seq'}, dimensions={0}, use_global_device_ids=true | all-gather | bytes 8448 | tf_op jit(solution)/shard_map/all_gather | solution.py:100
  80.1 25.7 %all-gather.5.cloned.1.call-done = bf16[4096,128]{1,0:T(8,128)(2,1)} async-done(((bf16[128,128]{1,0:T(8,128)(2,1)}), bf16[4096,128]{1,0:T(8,128)(2,1)}) %all-gather.5.cloned.1.call-update) | async-done | bytes 1048592 | tf_op jit(solution)/shard_map/all_gather | solution.py:98
  105.8 2.0 fusion.60
  108.3 63.3 %all-gather.7.cloned.1.call-done = bf16[4096,128]{1,0:T(8,128)(2,1)} async-done(((bf16[128,128]{1,0:T(8,128)(2,1)}), bf16[4096,128]{1,0:T(8,128)(2,1)}) %all-gather.7.cloned.1.call-update) | async-done | bytes 1048592 | tf_op jit(solution)/shard_map/all_gather | solution.py:99
  171.6 2.0 convolution_convert_fusion
  174.5 75.3 %reduce-scatter.4.cloned.1.call-done = bf16[128,128]{1,0:T(8,128)(2,1)} async-done(((bf16[1024,128]{1,0:T(8,128)(2,1)}), bf16[128,128]{1,0:T(8,128)(2,1)}) %reduce-scatter.4.cloned.1.call-update) | async-done | bytes 32784
  251.7 39.7 %psum.7 = bf16[128,128]{1,0:T(8,128)(2,1)S(1)} all-reduce(bf16[128,128]{1,0:T(8,128)(2,1)S(1)} %convolution_convert_fusion.2), channel_id=1, replica_groups=mesh['seq'=32,'band'=8] {'band'}, use_global_device_ids=true, to_apply=%region_4.0 | all-reduce | flops 16384 | bytes 65536 | tf_op jit(solution)/shard_map/psum | solution.py:135
  292.3 34.7 %all-gather = bf16[1024,128]{1,0:T(8,128)(2,1)S(1)} all-gather(bf16[128,128]{1,0:T(8,128)(2,1)S(1)} %convolution_convert_fusion.1), channel_id=2, replica_groups=mesh['seq'=32,'band'=8] {'band'}, dimensions={0}, use_global_device_ids=true | all-gather | bytes 294912 | tf_op jit(solution)/shard_map/all_gather | solution.py:140
  327.1 1.9 collective-permute-start
  330.6 5.7 %collective-permute-start.1 = (bf16[256,128]{1,0:T(8,128)(2,1)S(1)}, bf16[256,128]{1,0:T(8,128)(2,1)S(1)}, u32[]{:S(2)}, u32[]{:S(2)}) collective-permute-start(bf16[256,128]{1,0:T(8,128)(2,1)S(1)} %pad_maximum_fusion.9), channel_id=1, source_target_pairs={{8,0},{16,8},{24,16},{32,24},{40,32},{48,40},{56,48},{64,56},{72,6... | collective-permute-start | bytes 196616 | tf_op jit(solution)/shard_map/while/body/eval_jaxpr/ppermute | solution.py:16
  339.0 2.7 slice.172
  341.8 7.8 %reshape.195 = bf16[128,161,128]{2,1,0:T(8,128)(2,1)} reshape(bf16[20608,128]{1,0:T(8,128)(2,1)} %slice.172) | data formatting | bytes 10551296 | tf_op jit(solution)/shard_map/reshape | solution.py:169
  354.3 1.9 collective-permute-start.2
  356.2 5.8 %collective-permute-start.3 = (bf16[2,32,128]{2,0,1:T(2,128)(2,1)S(1)}, bf16[2,32,128]{2,0,1:T(2,128)(2,1)S(1)}, u32[]{:S(2)}, u32[]{:S(2)}) collective-permute-start(bf16[2,32,128]{2,0,1:T(2,128)(2,1)S(1)} %get-tuple-element.27), channel_id=1, source_target_pairs={{8,0},{16,8},{24,16},{32,24},{40,32},{48,40},{56,48},{64,56},{72,6... | collective-permute-start | bytes 49160 | tf_op jit(solution)/shard_map/ppermute | solution.py:27
  366.7 5.8 %collective-permute-done.4 = bf16[132,2,128]{2,0,1:T(8,128)(2,1)S(1)} collective-permute-done((bf16[132,2,128]{2,0,1:T(8,128)(2,1)S(1)}, bf16[132,2,128]{2,0,1:T(8,128)(2,1)S(1)}, u32[]{:S(2)}, u32[]{:S(2)}) %collective-permute-start.4) | collective-permute-done | bytes 67616 | tf_op jit(solution)/shard_map/ppermute | solution.py:27
  374.5 1.9 constant_dynamic-update-slice_fusion
  378.6 3.6 fusion.14
  383.3 1.9 collective-permute-start.6
  385.2 5.8 %collective-permute-start.7 = (bf16[4,32,128]{2,0,1:T(4,128)(2,1)S(1)}, bf16[4,32,128]{2,0,1:T(4,128)(2,1)S(1)}, u32[]{:S(2)}, u32[]{:S(2)}) collective-permute-start(bf16[4,32,128]{2,0,1:T(4,128)(2,1)S(1)} %get-tuple-element.25), channel_id=1, source_target_pairs={{8,0},{16,8},{24,16},{32,24},{40,32},{48,40},{56,48},{64,56},{72,6... | collective-permute-start | bytes 98312 | tf_op jit(solution)/shard_map/ppermute | solution.py:27
  392.6 5.7 %collective-permute-start.9 = (bf16[136,4,128]{2,0,1:T(8,128)(2,1)S(1)}, bf16[136,4,128]{2,0,1:T(8,128)(2,1)S(1)}, u32[]{:S(2)}, u32[]{:S(2)}) collective-permute-start(bf16[136,4,128]{2,0,1:T(8,128)(2,1)S(1)} %get-tuple-element.14), channel_id=1, source_target_pairs={{0,1},{1,2},{2,3},{3,4},{4,5},{5,6},{6,7},{8,9},{9,10},{10,11},{11... | collective-permute-start | bytes 417800 | tf_op jit(solution)/shard_map/ppermute | solution.py:26
  400.9 5.9 %collective-permute-done.8 = bf16[136,4,128]{2,0,1:T(8,128)(2,1)S(1)} collective-permute-done((bf16[136,4,128]{2,0,1:T(8,128)(2,1)S(1)}, bf16[136,4,128]{2,0,1:T(8,128)(2,1)S(1)}, u32[]{:S(2)}, u32[]{:S(2)}) %collective-permute-start.8) | collective-permute-done | bytes 139296 | tf_op jit(solution)/shard_map/ppermute | solution.py:27
  412.4 3.5 multiply_reduce_fusion
  (90 shorter events, 35.6 us)
Async XLA Ops:
  7.2 98.6 %copy-start = (bf16[1024,128]{1,0:T(8,128)(2,1)S(1)}, bf16[1024,128]{1,0:T(8,128)(2,1)}, u32[]{:S(2)}) copy-start(bf16[1024,128]{1,0:T(8,128)(2,1)} %param.16) | copy-start | bytes 786436
  7.2 98.6 %all-gather.5.cloned.1.call-start = ((), (), s32[]{:S(2)}) async-start(), calls=%async_computation.1 | async-start | bytes 1081344 | tf_op jit(solution)/shard_map/all_gather | solution.py:98
  41.5 130.1 %all-gather.7.cloned.1.call-start = ((), (), s32[]{:S(2)}) async-start(), calls=%async_computation.2 | async-start | bytes 1081344 | tf_op jit(solution)/shard_map/all_gather | solution.py:99
  43.4 206.4 %reduce-scatter.4.cloned.1.call-start = ((), (), s32[]{:S(2)}) async-start(), calls=%async_computation.3 | async-start | bytes 294912
  105.8 65.8 %copy-start.3 = (bf16[128,1024]{1,0:T(8,128)(2,1)S(1)}, bf16[128,1024]{1,0:T(8,128)(2,1)}, u32[]{:S(2)}) copy-start(bf16[128,1024]{1,0:T(8,128)(2,1)} %param.19) | copy-start | bytes 786436
  171.6 2.9 copy-start.7
  171.6 2.9 copy-start.1
  171.6 79.2 %copy-start.4 = (bf16[128,128]{1,0:T(8,128)(2,1)S(1)}, bf16[128,128]{1,0:T(8,128)(2,1)}, u32[]{:S(2)}) copy-start(bf16[128,128]{1,0:T(8,128)(2,1)} %param.13) | copy-start | bytes 98308
  173.5 162.8 %copy-start.5 = (f32[2,128]{1,0:T(2,128)S(1)}, f32[2,128]{1,0:T(2,128)}, u32[]{:S(2)}) copy-start(f32[2,128]{1,0:T(2,128)} %param.22) | copy-start | bytes 3076
  250.8 88.3 %copy-start.2 = (bf16[128,128]{1,0:T(8,128)(2,1)}, bf16[128,128]{1,0:T(8,128)(2,1)S(1)}, u32[]{:S(2)}) copy-start(bf16[128,128]{1,0:T(8,128)(2,1)S(1)} %add_convert_fusion) | copy-start | bytes 98308
  327.1 3.5 collective-permute-start
  330.6 7.6 %collective-permute-start.1 = (bf16[256,128]{1,0:T(8,128)(2,1)S(1)}, bf16[256,128]{1,0:T(8,128)(2,1)S(1)}, u32[]{:S(2)}, u32[]{:S(2)}) collective-permute-start(bf16[256,128]{1,0:T(8,128)(2,1)S(1)} %pad_maximum_fusion.9), channel_id=1, source_target_pairs={{8,0},{16,8},{24,16},{32,24},{40,32},{48,40},{56,48},{64,56},{72,6... | collective-permute-start | bytes 196616 | tf_op jit(solution)/shard_map/while/body/eval_jaxpr/ppermute | solution.py:16
  350.8 11.2 %copy-start.6 = (f32[2,128]{1,0:T(2,128)S(1)}, f32[2,128]{1,0:T(2,128)}, u32[]{:S(2)}) copy-start(f32[2,128]{1,0:T(2,128)} %param.24) | copy-start | bytes 3076
  354.3 7.8 %collective-permute-start.2 = (bf16[2,32,128]{2,0,1:T(2,128)(2,1)S(1)}, bf16[2,32,128]{2,0,1:T(2,128)(2,1)S(1)}, u32[]{:S(2)}, u32[]{:S(2)}) collective-permute-start(bf16[2,32,128]{2,0,1:T(2,128)(2,1)S(1)} %get-tuple-element.28), channel_id=1, source_target_pairs={{0,8},{8,16},{16,24},{24,32},{32,40},{40,48},{48,56},{56,64},{64,7... | collective-permute-start | bytes 49160 | tf_op jit(solution)/shard_map/ppermute | solution.py:26
  356.2 7.2 %collective-permute-start.3 = (bf16[2,32,128]{2,0,1:T(2,128)(2,1)S(1)}, bf16[2,32,128]{2,0,1:T(2,128)(2,1)S(1)}, u32[]{:S(2)}, u32[]{:S(2)}) collective-permute-start(bf16[2,32,128]{2,0,1:T(2,128)(2,1)S(1)} %get-tuple-element.27), channel_id=1, source_target_pairs={{8,0},{16,8},{24,16},{32,24},{40,32},{48,40},{56,48},{64,56},{72,6... | collective-permute-start | bytes 49160 | tf_op jit(solution)/shard_map/ppermute | solution.py:27
  363.5 3.2 collective-permute-start.5
  364.8 7.7 %collective-permute-start.4 = (bf16[132,2,128]{2,0,1:T(8,128)(2,1)S(1)}, bf16[132,2,128]{2,0,1:T(8,128)(2,1)S(1)}, u32[]{:S(2)}, u32[]{:S(2)}) collective-permute-start(bf16[132,2,128]{2,0,1:T(8,128)(2,1)S(1)} %get-tuple-element.24), channel_id=1, source_target_pairs={{1,0},{2,1},{3,2},{4,3},{5,4},{6,5},{7,6},{9,8},{10,9},{11,10},{12... | collective-permute-start | bytes 202760 | tf_op jit(solution)/shard_map/ppermute | solution.py:27
  383.3 7.7 %collective-permute-start.6 = (bf16[4,32,128]{2,0,1:T(4,128)(2,1)S(1)}, bf16[4,32,128]{2,0,1:T(4,128)(2,1)S(1)}, u32[]{:S(2)}, u32[]{:S(2)}) collective-permute-start(bf16[4,32,128]{2,0,1:T(4,128)(2,1)S(1)} %get-tuple-element.26), channel_id=1, source_target_pairs={{0,8},{8,16},{16,24},{24,32},{32,40},{40,48},{48,56},{56,64},{64,7... | collective-permute-start | bytes 98312 | tf_op jit(solution)/shard_map/ppermute | solution.py:26
  385.2 7.3 %collective-permute-start.7 = (bf16[4,32,128]{2,0,1:T(4,128)(2,1)S(1)}, bf16[4,32,128]{2,0,1:T(4,128)(2,1)S(1)}, u32[]{:S(2)}, u32[]{:S(2)}) collective-permute-start(bf16[4,32,128]{2,0,1:T(4,128)(2,1)S(1)} %get-tuple-element.25), channel_id=1, source_target_pairs={{8,0},{16,8},{24,16},{32,24},{40,32},{48,40},{56,48},{64,56},{72,6... | collective-permute-start | bytes 98312 | tf_op jit(solution)/shard_map/ppermute | solution.py:27
  392.6 8.3 %collective-permute-start.9 = (bf16[136,4,128]{2,0,1:T(8,128)(2,1)S(1)}, bf16[136,4,128]{2,0,1:T(8,128)(2,1)S(1)}, u32[]{:S(2)}, u32[]{:S(2)}) collective-permute-start(bf16[136,4,128]{2,0,1:T(8,128)(2,1)S(1)} %get-tuple-element.14), channel_id=1, source_target_pairs={{0,1},{1,2},{2,3},{3,4},{4,5},{5,6},{6,7},{8,9},{9,10},{10,11},{11... | collective-permute-start | bytes 417800 | tf_op jit(solution)/shard_map/ppermute | solution.py:26
  398.4 8.5 %collective-permute-start.8 = (bf16[136,4,128]{2,0,1:T(8,128)(2,1)S(1)}, bf16[136,4,128]{2,0,1:T(8,128)(2,1)S(1)}, u32[]{:S(2)}, u32[]{:S(2)}) collective-permute-start(bf16[136,4,128]{2,0,1:T(8,128)(2,1)S(1)} %get-tuple-element.20), channel_id=1, source_target_pairs={{1,0},{2,1},{3,2},{4,3},{5,4},{6,5},{7,6},{9,8},{10,9},{11,10},{12... | collective-permute-start | bytes 417800 | tf_op jit(solution)/shard_map/ppermute | solution.py:27
  411.2 1.2 copy-start.8
Sparse Core Ops, SparseCore 0:
  41.6 64.1 all-gather.4
  108.2 63.2 all-gather.6
  175.4 74.4 reduce-scatter.3
